TPU v7x, 128 devices: a whole 4x4x4 slice. The times are simulated.
128 devices in a mesh: depth: 8 (over z, y_lo), height: 16 (over x, y_hi, core).
Axes of the slice: x: 4, y: 4 (y_hi: 2, y_lo: 2; y = y_hi * 2 + y_lo), z: 4, core: 2. Of those that a mesh axis runs over, the one named last changes fastest.
Arguments:
- volume: bfloat16 [32, 32, 128, 128], P(None, 'depth', 'height'), may hold values from -6 to 6
- filters_three: bfloat16 [27, 64, 32], replicated, may hold values from -0.21875 to 0.21875
- filters_four: bfloat16 [27, 128, 64], P(None, 'height'), may hold values from -0.15625 to 0.15625
- cotangent: bfloat16 [128, 16, 64, 64], P(None, 'depth', 'height'), may hold values from -6 to 6
Outputs:
- grad_volume: bfloat16 [32, 32, 128, 128], P(None, 'depth', 'height')
- grad_three: float32 [27, 64, 32], replicated
- grad_four: float32 [27, 128, 64], P(None, 'height')
All inputs are finite; a program needn't handle non-finite values.
Results may differ from a plain program's by a relative error of at most 0.023.
Values may be sent and summed in bfloat16 or wider, within the bound.
A program may use at most 256 MiB of HBM per device.

v0:
```python
import math
import jax
import jax.numpy as jnp
from jax import lax
from jax.sharding import PartitionSpec as P

TANH_SCALE = 0.7978845608028654
CUBIC_TERM = 0.044715


def extended_2(x, sides, width):
    for axis, dim in sides:
        size, length = (lax.axis_size(axis), x.shape[dim])
        up = [(i, (i + 1) % size) for i in range(size - 1)]
        down = [(j, i) for i, j in up]
        last = lax.slice_in_dim(x, length - width, length, axis=dim)
        first = lax.slice_in_dim(x, 0, width, axis=dim)
        before = lax.ppermute(last, axis, up)
        after = lax.ppermute(first, axis, down)
        x = jnp.concatenate([before, x, after], axis=dim)
    return x


def gelu_value(values_in):
    inner = jnp.tanh(TANH_SCALE * (values_in + CUBIC_TERM * values_in * values_in * values_in))
    return 0.5 * values_in * (1.0 + inner)


def gelu_slope(values_in):
    inner = jnp.tanh(TANH_SCALE * (values_in + CUBIC_TERM * values_in * values_in * values_in))
    return 0.5 * (1.0 + inner) + 0.5 * values_in * (1.0 - inner * inner) * TANH_SCALE * (
        1.0 + 3.0 * CUBIC_TERM * values_in * values_in
    )


def pad_width(values_in):
    return jnp.pad(values_in, ((0, 0), (0, 0), (0, 0), (1, 1)))


def forward_taps(padded, weights, depth_cells, height_cells, width_cells):
    running = jnp.zeros((weights.shape[1], depth_cells, height_cells, width_cells), jnp.float32)
    for first in range(3):
        for second in range(3):
            for third in range(3):
                window_piece = padded[
                    :,
                    first : first + depth_cells,
                    second : second + height_cells,
                    third : third + width_cells,
                ]
                running = running + jnp.einsum(
                    "oi,idhw->odhw",
                    weights[9 * first + 3 * second + third],
                    window_piece,
                    preferred_element_type=jnp.float32,
                )
    return running


def transpose_taps(padded, weights, depth_cells, height_cells, width_cells):
    running = jnp.zeros((weights.shape[2], depth_cells, height_cells, width_cells), jnp.float32)
    for first in range(3):
        for second in range(3):
            for third in range(3):
                window_piece = padded[
                    :,
                    2 - first : 2 - first + depth_cells,
                    2 - second : 2 - second + height_cells,
                    2 - third : 2 - third + width_cells,
                ]
                running = running + jnp.einsum(
                    "oi,odhw->idhw",
                    weights[9 * first + 3 * second + third],
                    window_piece,
                    preferred_element_type=jnp.float32,
                )
    return running


def weight_taps(delta, padded, depth_cells, height_cells, width_cells):
    collected = []
    for first in range(3):
        for second in range(3):
            for third in range(3):
                window_piece = padded[
                    :,
                    first : first + depth_cells,
                    second : second + height_cells,
                    third : third + width_cells,
                ]
                collected.append(
                    jnp.einsum(
                        "odhw,idhw->oi", delta, window_piece, preferred_element_type=jnp.float32
                    )
                )
    return jnp.stack(collected, axis=0)


def shards(volume, filters_three, filters_four, cotangent):
    channels_in, depth_cells, height_cells, width_cells = volume.shape
    depth_count = lax.axis_size("depth")
    height_count = lax.axis_size("height")
    scale_three = 1.0 / math.sqrt(
        depth_cells * depth_count * height_cells * height_count * width_cells
    )
    scale_four = 1.0 / math.sqrt(
        depth_cells * depth_count // 2 * (height_cells * height_count // 2) * (width_cells // 2)
    )
    half_depth = depth_cells // 2
    half_height = height_cells // 2
    half_width = width_cells // 2
    extended = extended_2(volume, (("depth", 1), ("height", 2)), 1)
    padded = pad_width(extended)
    act_three = forward_taps(padded, filters_three, depth_cells, height_cells, width_cells)
    channels_mid = act_three.shape[0]
    hidden = gelu_value(act_three).reshape(
        channels_mid, half_depth, 2, half_height, 2, half_width, 2
    )
    pooled = (jnp.sum(hidden, axis=(2, 4, 6)) * 0.125).astype(jnp.bfloat16)
    full_bank = lax.all_gather(filters_four, "height", axis=1, tiled=True)
    rimmed = extended_2(pooled, (("depth", 1), ("height", 2)), 1)
    pooled_pad = pad_width(rimmed)
    act_four = forward_taps(pooled_pad, full_bank, half_depth, half_height, half_width)
    delta_four = (cotangent.astype(jnp.float32) * gelu_slope(act_four)).astype(jnp.bfloat16)
    partial_four = weight_taps(delta_four, pooled_pad, half_depth, half_height, half_width)
    depth_summed = lax.psum(partial_four.astype(jnp.bfloat16), "depth")
    grad_four = (
        lax.psum_scatter(depth_summed, "height", scatter_dimension=1, tiled=True).astype(
            jnp.float32
        )
        * scale_four
    )
    delta_rim = extended_2(delta_four, (("depth", 1), ("height", 2)), 1)
    back_pooled = transpose_taps(
        pad_width(delta_rim), full_bank, half_depth, half_height, half_width
    )
    spread = (
        jnp.repeat(jnp.repeat(jnp.repeat(back_pooled, 2, axis=1), 2, axis=2), 2, axis=3) * 0.125
    )
    delta_three = (spread * gelu_slope(act_three)).astype(jnp.bfloat16)
    partial_three = weight_taps(delta_three, padded, depth_cells, height_cells, width_cells)
    grad_three = lax.psum(partial_three, ("depth", "height")) * scale_three
    delta_extended = extended_2(delta_three, (("depth", 1), ("height", 2)), 1)
    grad_volume = transpose_taps(
        pad_width(delta_extended), filters_three, depth_cells, height_cells, width_cells
    ).astype(jnp.bfloat16)
    return (grad_volume, grad_three, grad_four)


def solution(mesh):
    in_specs = (
        P(None, "depth", "height", None),
        P(),
        P(None, "height", None),
        P(None, "depth", "height", None),
    )
    out_specs = (P(None, "depth", "height", None), P(), P(None, "height", None))
    return jax.shard_map(shards, mesh=mesh, in_specs=in_specs, out_specs=out_specs, check_vma=False)
```

profile of v0, /device:TPU:6, one launch (start us, length us, event | category | flops | bytes accessed | tf_op | source)
XLA Modules:
  0.0 348.1 jit_solution(2866375884435285282)
XLA Ops:
  9.0 3.5 %collective-permute-start = (bf16[32,1,8,128]{3,0,2,1:T(8,128)(2,1)S(1)}, bf16[32,1,8,128]{3,0,2,1:T(8,128)(2,1)S(1)}, u32[]{:S(2)}, u32[]{:S(2)}) collective-permute-start(bf16[32,1,8,128]{3,0,2,1:T(8,128)(2,1)S(1)} %copy.321), channel_id=1, source_target_pairs={{0,16},{16,32},{32,48},{48,64},{64,80},{80,96},{96,112},{1,17},{17... | collective-permute-start | bytes 196616 | tf_op jit(solution)/shard_map/ppermute | solution.py:18
  15.6 3.1 collective-permute-done.1
  18.8 1.9 collective-permute-start.2
  20.7 6.0 %collective-permute-start.3 = (bf16[32,6,1,128]{3,0,2,1:T(8,128)(2,1)S(1)}, bf16[32,6,1,128]{3,0,2,1:T(8,128)(2,1)S(1)}, u32[]{:S(2)}, u32[]{:S(2)}) collective-permute-start(bf16[32,6,1,128]{3,0,2,1:T(8,128)(2,1)S(1)} %get-tuple-element.19), channel_id=1, source_target_pairs={{1,0},{2,1},{3,2},{4,3},{5,4},{6,5},{7,6},{8,7},{9,8},{10,9},{11,1... | collective-permute-start | bytes 147464 | tf_op jit(solution)/shard_map/ppermute | solution.py:19
  38.3 2.0 add_multiply_fusion
  40.4 1.8 copy.91
  42.2 2.4 reduce_sum.9
  45.6 4.6 %collective-permute-start.4 = (bf16[64,1,4,64]{0,3,2,1:T(8,128)(2,1)S(1)}, bf16[64,1,4,64]{0,3,2,1:T(8,128)(2,1)S(1)}, u32[]{:S(2)}, u32[]{:S(2)}) collective-permute-start(bf16[64,1,4,64]{0,3,2,1:T(8,128)(2,1)S(1)} %get-tuple-element.33), channel_id=1, source_target_pairs={{0,16},{16,32},{32,48},{48,64},{64,80},{80,96},{96,112},{1,17},{17... | collective-permute-start | bytes 98312 | tf_op jit(solution)/shard_map/ppermute | solution.py:18
  51.5 23.7 %all_gather.3 = bf16[27,128,64]{2,1,0:T(8,128)(2,1)S(1)} all-gather(bf16[27,8,64]{2,1,0:T(8,128)(2,1)S(1)} %copy-done.14), channel_id=1, replica_groups=mesh['depth'=8,'height'=16] {'height'}, dimensions={1}, use_global_device_ids=true | all-gather | bytes 470016 | tf_op jit(solution)/shard_map/all_gather | solution.py:120
  75.2 2.3 collective-permute-start.6
  77.5 5.7 %collective-permute-start.7 = (bf16[64,4,1,64]{0,3,2,1:T(8,128)(2,1)S(1)}, bf16[64,4,1,64]{0,3,2,1:T(8,128)(2,1)S(1)}, u32[]{:S(2)}, u32[]{:S(2)}) collective-permute-start(bf16[64,4,1,64]{0,3,2,1:T(8,128)(2,1)S(1)} %get-tuple-element.25), channel_id=1, source_target_pairs={{1,0},{2,1},{3,2},{4,3},{5,4},{6,5},{7,6},{8,7},{9,8},{10,9},{11,1... | collective-permute-start | bytes 98312 | tf_op jit(solution)/shard_map/ppermute | solution.py:19
  96.6 4.0 %collective-permute-start.8 = (bf16[128,1,4,64]{0,3,2,1:T(8,128)(2,1)S(1)}, bf16[128,1,4,64]{0,3,2,1:T(8,128)(2,1)S(1)}, u32[]{:S(2)}, u32[]{:S(2)}) collective-permute-start(bf16[128,1,4,64]{0,3,2,1:T(8,128)(2,1)S(1)} %get-tuple-element.31), channel_id=1, source_target_pairs={{0,16},{16,32},{32,48},{48,64},{64,80},{80,96},{96,112},{1,17},{17... | collective-permute-start | bytes 196616 | tf_op jit(solution)/shard_map/ppermute | solution.py:18
  102.9 4.1 %collective-permute-done.9 = bf16[128,1,4,64]{0,3,2,1:T(8,128)(2,1)S(1)} collective-permute-done((bf16[128,1,4,64]{0,3,2,1:T(8,128)(2,1)S(1)}, bf16[128,1,4,64]{0,3,2,1:T(8,128)(2,1)S(1)}, u32[]{:S(2)}, u32[]{:S(2)}) %collective-permute-start.9) | collective-permute-done | bytes 65568 | tf_op jit(solution)/shard_map/ppermute | solution.py:19
  107.1 4.9 %collective-permute-start.11 = (bf16[128,4,1,64]{0,3,2,1:T(8,128)(2,1)S(1)}, bf16[128,4,1,64]{0,3,2,1:T(8,128)(2,1)S(1)}, u32[]{:S(2)}, u32[]{:S(2)}) collective-permute-start(bf16[128,4,1,64]{0,3,2,1:T(8,128)(2,1)S(1)} %get-tuple-element.23), channel_id=1, source_target_pairs={{1,0},{2,1},{3,2},{4,3},{5,4},{6,5},{7,6},{8,7},{9,8},{10,9},{11,1... | collective-permute-start | bytes 196616 | tf_op jit(solution)/shard_map/ppermute | solution.py:19
  112.0 1.9 collective-permute-start.10
  114.2 5.8 %collective-permute-done.10 = bf16[128,4,1,64]{0,3,2,1:T(8,128)(2,1)S(1)} collective-permute-done((bf16[128,4,1,64]{0,3,2,1:T(8,128)(2,1)S(1)}, bf16[128,4,1,64]{0,3,2,1:T(8,128)(2,1)S(1)}, u32[]{:S(2)}, u32[]{:S(2)}) %collective-permute-start.10) | collective-permute-done | bytes 65568 | tf_op jit(solution)/shard_map/ppermute | solution.py:18
  127.0 2.2 copy.120
  129.2 1.9 fusion.210
  140.7 3.3 copy.149
  145.6 4.6 %collective-permute-start.12 = (bf16[64,1,8,128]{3,0,2,1:T(8,128)(2,1)S(1)}, bf16[64,1,8,128]{3,0,2,1:T(8,128)(2,1)S(1)}, u32[]{:S(2)}, u32[]{:S(2)}) collective-permute-start(bf16[64,1,8,128]{3,0,2,1:T(8,128)(2,1)S(1)} %get-tuple-element.16), channel_id=1, source_target_pairs={{0,16},{16,32},{32,48},{48,64},{64,80},{80,96},{96,112},{1,17},{17... | collective-permute-start | bytes 393224 | tf_op jit(solution)/shard_map/ppermute | solution.py:18
  150.1 134.6 %all-reduce.6.cloned.1.call-done = f32[27,64,32]{1,2,0:T(8,128)} async-done(((f32[27,64,32]{1,2,0:T(8,128)}), f32[27,64,32]{1,2,0:T(8,128)}) %all-reduce.6.cloned.1.call-update) | async-done | bytes 221200 | tf_op jit(solution)/shard_map/psum | solution.py:142
  286.6 1.9 collective-permute-start.14
  288.5 6.3 %collective-permute-start.15 = (bf16[64,6,1,128]{3,0,2,1:T(8,128)(2,1)S(1)}, bf16[64,6,1,128]{3,0,2,1:T(8,128)(2,1)S(1)}, u32[]{:S(2)}, u32[]{:S(2)}) collective-permute-start(bf16[64,6,1,128]{3,0,2,1:T(8,128)(2,1)S(1)} %get-tuple-element.15), channel_id=1, source_target_pairs={{1,0},{2,1},{3,2},{4,3},{5,4},{6,5},{7,6},{8,7},{9,8},{10,9},{11,1... | collective-permute-start | bytes 294920 | tf_op jit(solution)/shard_map/ppermute | solution.py:19
  306.6 33.3 %psum.16 = bf16[27,8,64]{2,0,1:T(8,128)(2,1)S(1)} all-reduce(bf16[27,8,64]{2,0,1:T(8,128)(2,1)} %reduce-scatter.2.cloned.1.call-done), channel_id=1, replica_groups=mesh['depth'=8,'height'=16] {'depth'}, use_global_device_ids=true, to_apply=%region_2.3 | all-reduce | flops 13824 | bytes 55296 | tf_op jit(solution)/shard_map/psum | solution.py:126
  (243 shorter events, 65.6 us)
Async XLA Ops:
  8.0 18.7 %copy-start = (bf16[32,4,8,128]{3,2,1,0:T(8,128)(2,1)S(1)}, bf16[32,4,8,128]{3,2,1,0:T(8,128)(2,1)}, u32[]{:S(2)}) copy-start(bf16[32,4,8,128]{3,2,1,0:T(8,128)(2,1)} %param.4) | copy-start | bytes 786436
  8.0 18.7 %copy-start.6 = (bf16[27,64,32]{1,2,0:T(8,128)(2,1)S(1)}, bf16[27,64,32]{1,2,0:T(8,128)(2,1)}, u32[]{:S(2)}) copy-start(bf16[27,64,32]{1,2,0:T(8,128)(2,1)} %param.5) | copy-start | bytes 331780
  8.0 276.7 %all-reduce.6.cloned.1.call-start = ((), (), s32[]{:S(2)}) async-start(), calls=%async_computation.1 | async-start | bytes 884736 | tf_op jit(solution)/shard_map/psum | solution.py:142
  9.0 5.4 %collective-permute-start = (bf16[32,1,8,128]{3,0,2,1:T(8,128)(2,1)S(1)}, bf16[32,1,8,128]{3,0,2,1:T(8,128)(2,1)S(1)}, u32[]{:S(2)}, u32[]{:S(2)}) collective-permute-start(bf16[32,1,8,128]{3,0,2,1:T(8,128)(2,1)S(1)} %copy.321), channel_id=1, source_target_pairs={{0,16},{16,32},{32,48},{48,64},{64,80},{80,96},{96,112},{1,17},{17... | collective-permute-start | bytes 196616 | tf_op jit(solution)/shard_map/ppermute | solution.py:18
  12.5 6.2 %collective-permute-start.1 = (bf16[32,1,8,128]{3,0,2,1:T(8,128)(2,1)S(1)}, bf16[32,1,8,128]{3,0,2,1:T(8,128)(2,1)S(1)}, u32[]{:S(2)}, u32[]{:S(2)}) collective-permute-start(bf16[32,1,8,128]{3,0,2,1:T(8,128)(2,1)S(1)} %copy.322), channel_id=1, source_target_pairs={{16,0},{32,16},{48,32},{64,48},{80,64},{96,80},{112,96},{17,1},{33... | collective-permute-start | bytes 196616 | tf_op jit(solution)/shard_map/ppermute | solution.py:19
  15.6 19.9 %copy-start.4 = (bf16[32,5,8,128]{3,0,2,1:T(8,128)(2,1)}, bf16[32,5,8,128]{3,0,2,1:T(8,128)(2,1)S(1)}, u32[]{:S(2)}) copy-start(bf16[32,5,8,128]{3,0,2,1:T(8,128)(2,1)S(1)} %get-tuple-element.28) | copy-start | bytes 983044
  18.7 19.6 %copy-start.2 = (bf16[32,5,8,128]{3,0,2,1:T(8,128)(2,1)}, bf16[32,5,8,128]{3,0,2,1:T(8,128)(2,1)S(1)}, u32[]{:S(2)}) copy-start(bf16[32,5,8,128]{3,0,2,1:T(8,128)(2,1)S(1)} %get-tuple-element.35) | copy-start | bytes 983044
  18.8 8.3 %collective-permute-start.2 = (bf16[32,6,1,128]{3,0,2,1:T(8,128)(2,1)S(1)}, bf16[32,6,1,128]{3,0,2,1:T(8,128)(2,1)S(1)}, u32[]{:S(2)}, u32[]{:S(2)}) collective-permute-start(bf16[32,6,1,128]{3,0,2,1:T(8,128)(2,1)S(1)} %get-tuple-element.18), channel_id=1, source_target_pairs={{0,1},{1,2},{2,3},{3,4},{4,5},{5,6},{6,7},{7,8},{8,9},{9,10},{10,1... | collective-permute-start | bytes 147464 | tf_op jit(solution)/shard_map/ppermute | solution.py:18
  20.7 7.8 %collective-permute-start.3 = (bf16[32,6,1,128]{3,0,2,1:T(8,128)(2,1)S(1)}, bf16[32,6,1,128]{3,0,2,1:T(8,128)(2,1)S(1)}, u32[]{:S(2)}, u32[]{:S(2)}) collective-permute-start(bf16[32,6,1,128]{3,0,2,1:T(8,128)(2,1)S(1)} %get-tuple-element.19), channel_id=1, source_target_pairs={{1,0},{2,1},{3,2},{4,3},{5,4},{6,5},{7,6},{8,7},{9,8},{10,9},{11,1... | collective-permute-start | bytes 147464 | tf_op jit(solution)/shard_map/ppermute | solution.py:19
  27.1 9.8 %copy-start.10 = (bf16[32,6,1,128]{3,0,2,1:T(8,128)(2,1)}, bf16[32,6,1,128]{3,0,2,1:T(8,128)(2,1)S(1)}, u32[]{:S(2)}) copy-start(bf16[32,6,1,128]{3,0,2,1:T(8,128)(2,1)S(1)} %collective-permute-done.2) | copy-start | bytes 147460
  28.5 9.5 %copy-start.8 = (bf16[32,6,1,128]{3,0,2,1:T(8,128)(2,1)}, bf16[32,6,1,128]{3,0,2,1:T(8,128)(2,1)S(1)}, u32[]{:S(2)}) copy-start(bf16[32,6,1,128]{3,0,2,1:T(8,128)(2,1)S(1)} %collective-permute-done.3) | copy-start | bytes 147460
  45.6 29.6 %collective-permute-start.4 = (bf16[64,1,4,64]{0,3,2,1:T(8,128)(2,1)S(1)}, bf16[64,1,4,64]{0,3,2,1:T(8,128)(2,1)S(1)}, u32[]{:S(2)}, u32[]{:S(2)}) collective-permute-start(bf16[64,1,4,64]{0,3,2,1:T(8,128)(2,1)S(1)} %get-tuple-element.33), channel_id=1, source_target_pairs={{0,16},{16,32},{32,48},{48,64},{64,80},{80,96},{96,112},{1,17},{17... | collective-permute-start | bytes 98312 | tf_op jit(solution)/shard_map/ppermute | solution.py:18
  50.2 25.0 %collective-permute-start.5 = (bf16[64,1,4,64]{0,3,2,1:T(8,128)(2,1)S(1)}, bf16[64,1,4,64]{0,3,2,1:T(8,128)(2,1)S(1)}, u32[]{:S(2)}, u32[]{:S(2)}) collective-permute-start(bf16[64,1,4,64]{0,3,2,1:T(8,128)(2,1)S(1)} %get-tuple-element.34), channel_id=1, source_target_pairs={{16,0},{32,16},{48,32},{64,48},{80,64},{96,80},{112,96},{17,1},{33... | collective-permute-start | bytes 98312 | tf_op jit(solution)/shard_map/ppermute | solution.py:19
  75.2 8.2 %collective-permute-start.6 = (bf16[64,4,1,64]{0,3,2,1:T(8,128)(2,1)S(1)}, bf16[64,4,1,64]{0,3,2,1:T(8,128)(2,1)S(1)}, u32[]{:S(2)}, u32[]{:S(2)}) collective-permute-start(bf16[64,4,1,64]{0,3,2,1:T(8,128)(2,1)S(1)} %get-tuple-element.24), channel_id=1, source_target_pairs={{0,1},{1,2},{2,3},{3,4},{4,5},{5,6},{6,7},{7,8},{8,9},{9,10},{10,1... | collective-permute-start | bytes 98312 | tf_op jit(solution)/shard_map/ppermute | solution.py:18
  77.5 7.6 %collective-permute-start.7 = (bf16[64,4,1,64]{0,3,2,1:T(8,128)(2,1)S(1)}, bf16[64,4,1,64]{0,3,2,1:T(8,128)(2,1)S(1)}, u32[]{:S(2)}, u32[]{:S(2)}) collective-permute-start(bf16[64,4,1,64]{0,3,2,1:T(8,128)(2,1)S(1)} %get-tuple-element.25), channel_id=1, source_target_pairs={{1,0},{2,1},{3,2},{4,3},{5,4},{6,5},{7,6},{8,7},{9,8},{10,9},{11,1... | collective-permute-start | bytes 98312 | tf_op jit(solution)/shard_map/ppermute | solution.py:19
  96.6 6.4 %collective-permute-start.8 = (bf16[128,1,4,64]{0,3,2,1:T(8,128)(2,1)S(1)}, bf16[128,1,4,64]{0,3,2,1:T(8,128)(2,1)S(1)}, u32[]{:S(2)}, u32[]{:S(2)}) collective-permute-start(bf16[128,1,4,64]{0,3,2,1:T(8,128)(2,1)S(1)} %get-tuple-element.31), channel_id=1, source_target_pairs={{0,16},{16,32},{32,48},{48,64},{64,80},{80,96},{96,112},{1,17},{17... | collective-permute-start | bytes 196616 | tf_op jit(solution)/shard_map/ppermute | solution.py:18
  100.5 6.5 %collective-permute-start.9 = (bf16[128,1,4,64]{0,3,2,1:T(8,128)(2,1)S(1)}, bf16[128,1,4,64]{0,3,2,1:T(8,128)(2,1)S(1)}, u32[]{:S(2)}, u32[]{:S(2)}) collective-permute-start(bf16[128,1,4,64]{0,3,2,1:T(8,128)(2,1)S(1)} %get-tuple-element.32), channel_id=1, source_target_pairs={{16,0},{32,16},{48,32},{64,48},{80,64},{96,80},{112,96},{17,1},{33... | collective-permute-start | bytes 196616 | tf_op jit(solution)/shard_map/ppermute | solution.py:19
  107.1 7.1 %collective-permute-start.11 = (bf16[128,4,1,64]{0,3,2,1:T(8,128)(2,1)S(1)}, bf16[128,4,1,64]{0,3,2,1:T(8,128)(2,1)S(1)}, u32[]{:S(2)}, u32[]{:S(2)}) collective-permute-start(bf16[128,4,1,64]{0,3,2,1:T(8,128)(2,1)S(1)} %get-tuple-element.23), channel_id=1, source_target_pairs={{1,0},{2,1},{3,2},{4,3},{5,4},{6,5},{7,6},{8,7},{9,8},{10,9},{11,1... | collective-permute-start | bytes 196616 | tf_op jit(solution)/shard_map/ppermute | solution.py:19
  112.0 8.0 %collective-permute-start.10 = (bf16[128,4,1,64]{0,3,2,1:T(8,128)(2,1)S(1)}, bf16[128,4,1,64]{0,3,2,1:T(8,128)(2,1)S(1)}, u32[]{:S(2)}, u32[]{:S(2)}) collective-permute-start(bf16[128,4,1,64]{0,3,2,1:T(8,128)(2,1)S(1)} %get-tuple-element.22), channel_id=1, source_target_pairs={{0,1},{1,2},{2,3},{3,4},{4,5},{5,6},{6,7},{7,8},{8,9},{9,10},{10,1... | collective-permute-start | bytes 196616 | tf_op jit(solution)/shard_map/ppermute | solution.py:18
  139.8 166.8 %reduce-scatter.2.cloned.1.call-start = ((), (), s32[]{:S(2)}) async-start(), calls=%async_computation.2 | async-start | bytes 1114112 | tf_op jit(solution)/shard_map/reduce_scatter | solution.py:128
  144.3 142.3 %collective-permute-start.13 = (bf16[64,1,8,128]{3,0,2,1:T(8,128)(2,1)S(1)}, bf16[64,1,8,128]{3,0,2,1:T(8,128)(2,1)S(1)}, u32[]{:S(2)}, u32[]{:S(2)}) collective-permute-start(bf16[64,1,8,128]{3,0,2,1:T(8,128)(2,1)S(1)} %get-tuple-element.17), channel_id=1, source_target_pairs={{16,0},{32,16},{48,32},{64,48},{80,64},{96,80},{112,96},{17,1},{33... | collective-permute-start | bytes 393224 | tf_op jit(solution)/shard_map/ppermute | solution.py:19
  145.6 141.0 %collective-permute-start.12 = (bf16[64,1,8,128]{3,0,2,1:T(8,128)(2,1)S(1)}, bf16[64,1,8,128]{3,0,2,1:T(8,128)(2,1)S(1)}, u32[]{:S(2)}, u32[]{:S(2)}) collective-permute-start(bf16[64,1,8,128]{3,0,2,1:T(8,128)(2,1)S(1)} %get-tuple-element.16), channel_id=1, source_target_pairs={{0,16},{16,32},{32,48},{48,64},{64,80},{80,96},{96,112},{1,17},{17... | collective-permute-start | bytes 393224 | tf_op jit(solution)/shard_map/ppermute | solution.py:18
  286.6 8.6 %collective-permute-start.14 = (bf16[64,6,1,128]{3,0,2,1:T(8,128)(2,1)S(1)}, bf16[64,6,1,128]{3,0,2,1:T(8,128)(2,1)S(1)}, u32[]{:S(2)}, u32[]{:S(2)}) collective-permute-start(bf16[64,6,1,128]{3,0,2,1:T(8,128)(2,1)S(1)} %get-tuple-element.14), channel_id=1, source_target_pairs={{0,1},{1,2},{2,3},{3,4},{4,5},{5,6},{6,7},{7,8},{8,9},{9,10},{10,1... | collective-permute-start | bytes 294920 | tf_op jit(solution)/shard_map/ppermute | solution.py:18
  288.5 8.2 %collective-permute-start.15 = (bf16[64,6,1,128]{3,0,2,1:T(8,128)(2,1)S(1)}, bf16[64,6,1,128]{3,0,2,1:T(8,128)(2,1)S(1)}, u32[]{:S(2)}, u32[]{:S(2)}) collective-permute-start(bf16[64,6,1,128]{3,0,2,1:T(8,128)(2,1)S(1)} %get-tuple-element.15), channel_id=1, source_target_pairs={{1,0},{2,1},{3,2},{4,3},{5,4},{6,5},{7,6},{8,7},{9,8},{10,9},{11,1... | collective-permute-start | bytes 294920 | tf_op jit(solution)/shard_map/ppermute | solution.py:19
  (10 other events, 30.4 us)
Sparse Core Ops, SparseCore 0:
  139.9 144.7 all-reduce.5
Sparse Core Ops, SparseCore 1:
  144.6 66.4 reduce-scatter.1
where the time goes:
time: 349 us; the launch traced here: 348 us
  waiting for transfers between devices  154 us (44%)
  blocking collectives  57 us (16%)
  starting transfers between devices  52.8 us (15%)
  matrix products  43.6 us (12%)
  between operations  16.6 us (5%)
  local copies, waits for them, and re-layouts  14.2 us (4%)
  other arithmetic  10.1 us (3%)
    psum x1, waiting for transfers between devices, shards(): grad_three = lax.psum(partial_three, ('depth', 'height')) * scale_three  135 us
    psum x1, blocking collectives, shards(): depth_summed = lax.psum(partial_four.astype(jnp.bfloat16), 'depth')  33.3 us
    ppermute x8, starting transfers between devices, extended_2(): after = lax.ppermute(first, axis, down)  28.1 us
    ppermute x8, starting transfers between devices, extended_2(): before = lax.ppermute(last, axis, up)  24.6 us
    all_gather x1, blocking collectives, shards(): full_bank = lax.all_gather(filters_four, 'height', axis=1, tiled=True)  23.7 us
    dot_general x54, matrix products, forward_taps(): jnp.einsum('oi,idhw->odhw', weights[9 * first + 3 * second + third], wind...  16.9 us
    dot_general x54, matrix products, weight_taps(): jnp.einsum('odhw,idhw->oi', delta, window_piece, preferred_element_type=j...  14.4 us
    dot_general x54, matrix products, transpose_taps(): jnp.einsum('oi,odhw->idhw', weights[9 * first + 3 * second + third], wind...  12.3 us
  transfers between devices with their start and end apart: 18, of which 9 were waited for; matrix products, arithmetic and copies ran while one was open for 5% of the time, Pallas kernels for 0%

commit v1 on v0

--- a/solution.py
+++ b/solution.py
@@ -139,7 +139,7 @@
     )
     delta_three = (spread * gelu_slope(act_three)).astype(jnp.bfloat16)
     partial_three = weight_taps(delta_three, padded, depth_cells, height_cells, width_cells)
-    grad_three = lax.psum(partial_three, ("depth", "height")) * scale_three
+    grad_three = lax.psum(lax.psum(partial_three, "height"), "depth") * scale_three
     delta_extended = extended_2(delta_three, (("depth", 1), ("height", 2)), 1)
     grad_volume = transpose_taps(
         pad_width(delta_extended), filters_three, depth_cells, height_cells, width_cells

time: 349 us -> 464 us (1.33)
  waiting for transfers between devices: 154 us -> 269 us
    reduce_scatter x1, waiting for transfers between devices: 0.01 us -> 67.6 us  [shards(): lax.psum_scatter(depth_summed, 'height', scatter_dimension=1, tiled=True)]
    psum x1 -> x2, waiting for transfers between devices: 135 us -> 181 us  [the longest x1 129 us: shards(): lax.psum(partial_three, 'height')]
  transfers between devices with their start and end apart: 18 -> 19, of which waited for: 9 -> 13; matrix products, arithmetic and copies ran while one was open for 5% -> 4% of each run, Pallas kernels for 0% -> 0%
where the time goes in v1:
time: 464 us; the launch traced here: 462 us
  waiting for transfers between devices  269 us (58%)
  blocking collectives  58.3 us (13%)
  starting transfers between devices  53 us (11%)
  matrix products  43.9 us (9%)
  between operations  14.9 us (3%)
  local copies, waits for them, and re-layouts  13.6 us (3%)
  other arithmetic  9.67 us (2%)
    psum x1, waiting for transfers between devices, shards(): lax.psum(partial_three, 'height')  129 us
    reduce_scatter x1, waiting for transfers between devices, shards(): lax.psum_scatter(depth_summed, 'height', scatter_dimension=1, tiled=True)  67.6 us
    psum x1, waiting for transfers between devices, shards(): lax.psum(lax.psum(partial_three, 'height'), 'depth') * scale_three  51.8 us
    psum x1, blocking collectives, shards(): depth_summed = lax.psum(partial_four.astype(jnp.bfloat16), 'depth')  34.8 us
    ppermute x8, starting transfers between devices, extended_2(): before = lax.ppermute(last, axis, up)  26.5 us
    ppermute x8, starting transfers between devices, extended_2(): after = lax.ppermute(first, axis, down)  26.4 us
    all_gather x1, blocking collectives, shards(): full_bank = lax.all_gather(filters_four, 'height', axis=1, tiled=True)  23.5 us
    dot_general x54, matrix products, forward_taps(): jnp.einsum('oi,idhw->odhw', weights[9 * first + 3 * second + third], wind...  16.8 us
  transfers between devices with their start and end apart: 19, of which 13 were waited for; matrix products, arithmetic and copies ran while one was open for 4% of the time, Pallas kernels for 0%

profile of v1, /device:TPU:6, one launch (start us, length us, event | category | flops | bytes accessed | tf_op | source)
XLA Modules:
  0.0 462.4 jit_solution(2288689977206829569)
XLA Ops:
  8.2 3.5 collective-permute-start
  14.8 3.1 collective-permute-done.1
  17.9 1.9 collective-permute-start.2
  19.8 6.0 %collective-permute-start.3 = (bf16[32,6,1,128]{3,0,2,1:T(8,128)(2,1)S(1)}, bf16[32,6,1,128]{3,0,2,1:T(8,128)(2,1)S(1)}, u32[]{:S(2)}, u32[]{:S(2)}) collective-permute-start(bf16[32,6,1,128]{3,0,2,1:T(8,128)(2,1)S(1)} %get-tuple-element.19), channel_id=1, source_target_pairs={{1,0},{2,1},{3,2},{4,3},{5,4},{6,5},{7,6},{8,7},{9,8},{10,9},{11,1... | collective-permute-start | bytes 147464 | tf_op jit(solution)/shard_map/ppermute | solution.py:19
  39.5 2.0 copy.91
  41.4 2.9 reduce_sum.9
  44.4 4.6 collective-permute-start.4
  50.4 23.5 %all_gather.3 = bf16[27,128,64]{2,1,0:T(8,128)(2,1)S(1)} all-gather(bf16[27,8,64]{2,1,0:T(8,128)(2,1)S(1)} %copy-done.16), channel_id=1, replica_groups=mesh['depth'=8,'height'=16] {'height'}, dimensions={1}, use_global_device_ids=true | all-gather | bytes 470016 | tf_op jit(solution)/shard_map/all_gather | solution.py:120
  73.9 2.3 collective-permute-start.6
  76.1 5.9 %collective-permute-start.7 = (bf16[64,4,1,64]{0,3,2,1:T(8,128)(2,1)S(1)}, bf16[64,4,1,64]{0,3,2,1:T(8,128)(2,1)S(1)}, u32[]{:S(2)}, u32[]{:S(2)}) collective-permute-start(bf16[64,4,1,64]{0,3,2,1:T(8,128)(2,1)S(1)} %get-tuple-element.25), channel_id=1, source_target_pairs={{1,0},{2,1},{3,2},{4,3},{5,4},{6,5},{7,6},{8,7},{9,8},{10,9},{11,1... | collective-permute-start | bytes 98312 | tf_op jit(solution)/shard_map/ppermute | solution.py:19
  94.7 3.9 collective-permute-start.8
  101.1 4.1 collective-permute-done.9
  105.2 4.9 %collective-permute-start.11 = (bf16[128,4,1,64]{0,3,2,1:T(8,128)(2,1)S(1)}, bf16[128,4,1,64]{0,3,2,1:T(8,128)(2,1)S(1)}, u32[]{:S(2)}, u32[]{:S(2)}) collective-permute-start(bf16[128,4,1,64]{0,3,2,1:T(8,128)(2,1)S(1)} %get-tuple-element.23), channel_id=1, source_target_pairs={{1,0},{2,1},{3,2},{4,3},{5,4},{6,5},{7,6},{8,7},{9,8},{10,9},{11,1... | collective-permute-start | bytes 196616 | tf_op jit(solution)/shard_map/ppermute | solution.py:19
  112.3 5.8 %collective-permute-done.10 = bf16[128,4,1,64]{0,3,2,1:T(8,128)(2,1)S(1)} collective-permute-done((bf16[128,4,1,64]{0,3,2,1:T(8,128)(2,1)S(1)}, bf16[128,4,1,64]{0,3,2,1:T(8,128)(2,1)S(1)}, u32[]{:S(2)}, u32[]{:S(2)}) %collective-permute-start.10) | collective-permute-done | bytes 65568 | tf_op jit(solution)/shard_map/ppermute | solution.py:18
  125.2 2.2 copy.120
  127.3 1.9 fusion.210
  139.1 128.7 %all-reduce.7.cloned.1.call-done = f32[27,64,32]{1,2,0:T(8,128)} async-done(((f32[27,64,32]{1,2,0:T(8,128)}), f32[27,64,32]{1,2,0:T(8,128)}) %all-reduce.7.cloned.1.call-update) | async-done | bytes 221200 | tf_op jit(solution)/shard_map/psum | solution.py:142
  268.1 2.5 copy.149
  272.0 4.6 collective-permute-start.12
  279.1 3.8 collective-permute-start.14
  282.9 4.4 collective-permute-start.15
  299.1 51.8 %all-reduce.9.cloned.1.call-done = f32[27,64,32]{1,2,0:T(8,128)} async-done(((f32[27,64,32]{1,2,0:T(8,128)}), f32[27,64,32]{1,2,0:T(8,128)}) %all-reduce.9.cloned.1.call-update) | async-done | bytes 221200 | tf_op jit(solution)/shard_map/psum | solution.py:142
  352.8 67.6 %reduce-scatter.2.cloned.1.call-done = bf16[27,8,64]{2,0,1:T(8,128)(2,1)} async-done(((bf16[27,128,64]{2,0,1:T(8,128)(2,1)}), bf16[27,8,64]{2,0,1:T(8,128)(2,1)}) %reduce-scatter.2.cloned.1.call-update) | async-done | bytes 27664 | tf_op jit(solution)/shard_map/reduce_scatter | solution.py:128
  420.3 34.8 %psum.24 = bf16[27,8,64]{2,0,1:T(8,128)(2,1)S(1)} all-reduce(bf16[27,8,64]{2,0,1:T(8,128)(2,1)} %reduce-scatter.2.cloned.1.call-done), channel_id=1, replica_groups=mesh['depth'=8,'height'=16] {'depth'}, use_global_device_ids=true, to_apply=%region_3.4 | all-reduce | flops 13824 | bytes 55296 | tf_op jit(solution)/shard_map/psum | solution.py:126
  (250 shorter events, 70.8 us)
Async XLA Ops:
  7.2 18.7 %copy-start = (bf16[32,4,8,128]{3,2,1,0:T(8,128)(2,1)S(1)}, bf16[32,4,8,128]{3,2,1,0:T(8,128)(2,1)}, u32[]{:S(2)}) copy-start(bf16[32,4,8,128]{3,2,1,0:T(8,128)(2,1)} %param.4) | copy-start | bytes 786436
  7.2 18.7 %copy-start.6 = (bf16[27,64,32]{1,2,0:T(8,128)(2,1)S(1)}, bf16[27,64,32]{1,2,0:T(8,128)(2,1)}, u32[]{:S(2)}) copy-start(bf16[27,64,32]{1,2,0:T(8,128)(2,1)} %param.5) | copy-start | bytes 331780
  7.2 260.6 %all-reduce.7.cloned.1.call-start = ((), (), s32[]{:S(2)}) async-start(), calls=%async_computation.1 | async-start | bytes 884736 | tf_op jit(solution)/shard_map/psum | solution.py:142
  8.2 5.4 %collective-permute-start = (bf16[32,1,8,128]{3,0,2,1:T(8,128)(2,1)S(1)}, bf16[32,1,8,128]{3,0,2,1:T(8,128)(2,1)S(1)}, u32[]{:S(2)}, u32[]{:S(2)}) collective-permute-start(bf16[32,1,8,128]{3,0,2,1:T(8,128)(2,1)S(1)} %copy.321), channel_id=1, source_target_pairs={{0,16},{16,32},{32,48},{48,64},{64,80},{80,96},{96,112},{1,17},{17... | collective-permute-start | bytes 196616 | tf_op jit(solution)/shard_map/ppermute | solution.py:18
  11.7 6.2 %collective-permute-start.1 = (bf16[32,1,8,128]{3,0,2,1:T(8,128)(2,1)S(1)}, bf16[32,1,8,128]{3,0,2,1:T(8,128)(2,1)S(1)}, u32[]{:S(2)}, u32[]{:S(2)}) collective-permute-start(bf16[32,1,8,128]{3,0,2,1:T(8,128)(2,1)S(1)} %copy.322), channel_id=1, source_target_pairs={{16,0},{32,16},{48,32},{64,48},{80,64},{96,80},{112,96},{17,1},{33... | collective-permute-start | bytes 196616 | tf_op jit(solution)/shard_map/ppermute | solution.py:19
  14.7 19.9 %copy-start.4 = (bf16[32,5,8,128]{3,0,2,1:T(8,128)(2,1)}, bf16[32,5,8,128]{3,0,2,1:T(8,128)(2,1)S(1)}, u32[]{:S(2)}) copy-start(bf16[32,5,8,128]{3,0,2,1:T(8,128)(2,1)S(1)} %get-tuple-element.28) | copy-start | bytes 983044
  17.9 19.9 %copy-start.2 = (bf16[32,5,8,128]{3,0,2,1:T(8,128)(2,1)}, bf16[32,5,8,128]{3,0,2,1:T(8,128)(2,1)S(1)}, u32[]{:S(2)}) copy-start(bf16[32,5,8,128]{3,0,2,1:T(8,128)(2,1)S(1)} %get-tuple-element.35) | copy-start | bytes 983044
  17.9 8.3 %collective-permute-start.2 = (bf16[32,6,1,128]{3,0,2,1:T(8,128)(2,1)S(1)}, bf16[32,6,1,128]{3,0,2,1:T(8,128)(2,1)S(1)}, u32[]{:S(2)}, u32[]{:S(2)}) collective-permute-start(bf16[32,6,1,128]{3,0,2,1:T(8,128)(2,1)S(1)} %get-tuple-element.18), channel_id=1, source_target_pairs={{0,1},{1,2},{2,3},{3,4},{4,5},{5,6},{6,7},{7,8},{8,9},{9,10},{10,1... | collective-permute-start | bytes 147464 | tf_op jit(solution)/shard_map/ppermute | solution.py:18
  19.8 7.8 %collective-permute-start.3 = (bf16[32,6,1,128]{3,0,2,1:T(8,128)(2,1)S(1)}, bf16[32,6,1,128]{3,0,2,1:T(8,128)(2,1)S(1)}, u32[]{:S(2)}, u32[]{:S(2)}) collective-permute-start(bf16[32,6,1,128]{3,0,2,1:T(8,128)(2,1)S(1)} %get-tuple-element.19), channel_id=1, source_target_pairs={{1,0},{2,1},{3,2},{4,3},{5,4},{6,5},{7,6},{8,7},{9,8},{10,9},{11,1... | collective-permute-start | bytes 147464 | tf_op jit(solution)/shard_map/ppermute | solution.py:19
  44.4 29.4 %collective-permute-start.4 = (bf16[64,1,4,64]{0,3,2,1:T(8,128)(2,1)S(1)}, bf16[64,1,4,64]{0,3,2,1:T(8,128)(2,1)S(1)}, u32[]{:S(2)}, u32[]{:S(2)}) collective-permute-start(bf16[64,1,4,64]{0,3,2,1:T(8,128)(2,1)S(1)} %get-tuple-element.33), channel_id=1, source_target_pairs={{0,16},{16,32},{32,48},{48,64},{64,80},{80,96},{96,112},{1,17},{17... | collective-permute-start | bytes 98312 | tf_op jit(solution)/shard_map/ppermute | solution.py:18
  49.1 24.8 %collective-permute-start.5 = (bf16[64,1,4,64]{0,3,2,1:T(8,128)(2,1)S(1)}, bf16[64,1,4,64]{0,3,2,1:T(8,128)(2,1)S(1)}, u32[]{:S(2)}, u32[]{:S(2)}) collective-permute-start(bf16[64,1,4,64]{0,3,2,1:T(8,128)(2,1)S(1)} %get-tuple-element.34), channel_id=1, source_target_pairs={{16,0},{32,16},{48,32},{64,48},{80,64},{96,80},{112,96},{17,1},{33... | collective-permute-start | bytes 98312 | tf_op jit(solution)/shard_map/ppermute | solution.py:19
  73.9 8.4 %collective-permute-start.6 = (bf16[64,4,1,64]{0,3,2,1:T(8,128)(2,1)S(1)}, bf16[64,4,1,64]{0,3,2,1:T(8,128)(2,1)S(1)}, u32[]{:S(2)}, u32[]{:S(2)}) collective-permute-start(bf16[64,4,1,64]{0,3,2,1:T(8,128)(2,1)S(1)} %get-tuple-element.24), channel_id=1, source_target_pairs={{0,1},{1,2},{2,3},{3,4},{4,5},{5,6},{6,7},{7,8},{8,9},{9,10},{10,1... | collective-permute-start | bytes 98312 | tf_op jit(solution)/shard_map/ppermute | solution.py:18
  76.1 7.6 %collective-permute-start.7 = (bf16[64,4,1,64]{0,3,2,1:T(8,128)(2,1)S(1)}, bf16[64,4,1,64]{0,3,2,1:T(8,128)(2,1)S(1)}, u32[]{:S(2)}, u32[]{:S(2)}) collective-permute-start(bf16[64,4,1,64]{0,3,2,1:T(8,128)(2,1)S(1)} %get-tuple-element.25), channel_id=1, source_target_pairs={{1,0},{2,1},{3,2},{4,3},{5,4},{6,5},{7,6},{8,7},{9,8},{10,9},{11,1... | collective-permute-start | bytes 98312 | tf_op jit(solution)/shard_map/ppermute | solution.py:19
  94.7 6.4 %collective-permute-start.8 = (bf16[128,1,4,64]{0,3,2,1:T(8,128)(2,1)S(1)}, bf16[128,1,4,64]{0,3,2,1:T(8,128)(2,1)S(1)}, u32[]{:S(2)}, u32[]{:S(2)}) collective-permute-start(bf16[128,1,4,64]{0,3,2,1:T(8,128)(2,1)S(1)} %get-tuple-element.31), channel_id=1, source_target_pairs={{0,16},{16,32},{32,48},{48,64},{64,80},{80,96},{96,112},{1,17},{17... | collective-permute-start | bytes 196616 | tf_op jit(solution)/shard_map/ppermute | solution.py:18
  98.7 6.5 %collective-permute-start.9 = (bf16[128,1,4,64]{0,3,2,1:T(8,128)(2,1)S(1)}, bf16[128,1,4,64]{0,3,2,1:T(8,128)(2,1)S(1)}, u32[]{:S(2)}, u32[]{:S(2)}) collective-permute-start(bf16[128,1,4,64]{0,3,2,1:T(8,128)(2,1)S(1)} %get-tuple-element.32), channel_id=1, source_target_pairs={{16,0},{32,16},{48,32},{64,48},{80,64},{96,80},{112,96},{17,1},{33... | collective-permute-start | bytes 196616 | tf_op jit(solution)/shard_map/ppermute | solution.py:19
  105.2 7.1 %collective-permute-start.11 = (bf16[128,4,1,64]{0,3,2,1:T(8,128)(2,1)S(1)}, bf16[128,4,1,64]{0,3,2,1:T(8,128)(2,1)S(1)}, u32[]{:S(2)}, u32[]{:S(2)}) collective-permute-start(bf16[128,4,1,64]{0,3,2,1:T(8,128)(2,1)S(1)} %get-tuple-element.23), channel_id=1, source_target_pairs={{1,0},{2,1},{3,2},{4,3},{5,4},{6,5},{7,6},{8,7},{9,8},{10,9},{11,1... | collective-permute-start | bytes 196616 | tf_op jit(solution)/shard_map/ppermute | solution.py:19
  110.2 8.0 %collective-permute-start.10 = (bf16[128,4,1,64]{0,3,2,1:T(8,128)(2,1)S(1)}, bf16[128,4,1,64]{0,3,2,1:T(8,128)(2,1)S(1)}, u32[]{:S(2)}, u32[]{:S(2)}) collective-permute-start(bf16[128,4,1,64]{0,3,2,1:T(8,128)(2,1)S(1)} %get-tuple-element.22), channel_id=1, source_target_pairs={{0,1},{1,2},{2,3},{3,4},{4,5},{5,6},{6,7},{7,8},{8,9},{9,10},{10,1... | collective-permute-start | bytes 196616 | tf_op jit(solution)/shard_map/ppermute | solution.py:18
  137.9 213.0 %all-reduce.9.cloned.1.call-start = ((), (), s32[]{:S(2)}) async-start(), calls=%async_computation.2 | async-start | bytes 884736 | tf_op jit(solution)/shard_map/psum | solution.py:142
  139.1 137.4 %copy-start.7 = (bf16[27,64,32]{1,2,0:T(8,128)(2,1)S(1)}, bf16[27,64,32]{1,2,0:T(8,128)(2,1)}, u32[]{:S(2)}) copy-start(bf16[27,64,32]{1,2,0:T(8,128)(2,1)} %param.5) | copy-start | bytes 331780
  267.9 152.5 %reduce-scatter.2.cloned.1.call-start = ((), (), s32[]{:S(2)}) async-start(), calls=%async_computation.3 | async-start | bytes 1114112 | tf_op jit(solution)/shard_map/reduce_scatter | solution.py:128
  270.7 6.9 %collective-permute-start.13 = (bf16[64,1,8,128]{3,0,2,1:T(8,128)(2,1)S(1)}, bf16[64,1,8,128]{3,0,2,1:T(8,128)(2,1)S(1)}, u32[]{:S(2)}, u32[]{:S(2)}) collective-permute-start(bf16[64,1,8,128]{3,0,2,1:T(8,128)(2,1)S(1)} %get-tuple-element.17), channel_id=1, source_target_pairs={{16,0},{32,16},{48,32},{64,48},{80,64},{96,80},{112,96},{17,1},{33... | collective-permute-start | bytes 393224 | tf_op jit(solution)/shard_map/ppermute | solution.py:19
  272.0 7.1 %collective-permute-start.12 = (bf16[64,1,8,128]{3,0,2,1:T(8,128)(2,1)S(1)}, bf16[64,1,8,128]{3,0,2,1:T(8,128)(2,1)S(1)}, u32[]{:S(2)}, u32[]{:S(2)}) collective-permute-start(bf16[64,1,8,128]{3,0,2,1:T(8,128)(2,1)S(1)} %get-tuple-element.16), channel_id=1, source_target_pairs={{0,16},{16,32},{32,48},{48,64},{64,80},{80,96},{96,112},{1,17},{17... | collective-permute-start | bytes 393224 | tf_op jit(solution)/shard_map/ppermute | solution.py:18
  279.1 8.6 %collective-permute-start.14 = (bf16[64,6,1,128]{3,0,2,1:T(8,128)(2,1)S(1)}, bf16[64,6,1,128]{3,0,2,1:T(8,128)(2,1)S(1)}, u32[]{:S(2)}, u32[]{:S(2)}) collective-permute-start(bf16[64,6,1,128]{3,0,2,1:T(8,128)(2,1)S(1)} %get-tuple-element.14), channel_id=1, source_target_pairs={{0,1},{1,2},{2,3},{3,4},{4,5},{5,6},{6,7},{7,8},{8,9},{9,10},{10,1... | collective-permute-start | bytes 294920 | tf_op jit(solution)/shard_map/ppermute | solution.py:18
  282.9 6.4 %collective-permute-start.15 = (bf16[64,6,1,128]{3,0,2,1:T(8,128)(2,1)S(1)}, bf16[64,6,1,128]{3,0,2,1:T(8,128)(2,1)S(1)}, u32[]{:S(2)}, u32[]{:S(2)}) collective-permute-start(bf16[64,6,1,128]{3,0,2,1:T(8,128)(2,1)S(1)} %get-tuple-element.15), channel_id=1, source_target_pairs={{1,0},{2,1},{3,2},{4,3},{5,4},{6,5},{7,6},{8,7},{9,8},{10,9},{11,1... | collective-permute-start | bytes 294920 | tf_op jit(solution)/shard_map/ppermute | solution.py:19
  (13 other events, 50.1 us)
Sparse Core Ops, SparseCore 0:
  138.1 129.7 all-reduce.6
  270.5 80.4 all-reduce.8
  354.8 65.4 reduce-scatter.1
